TPU v7x, 512 devices: a whole 4x8x8 slice. The times are simulated.
512 devices in a mesh: ctx: 32 (over x, y), tp: 16 (over z, core).
Axes of the slice: x: 4, y: 8, z: 8, core: 2. Of those that a mesh axis runs over, the one named last changes fastest.
Arguments:
- prefix_x: bfloat16 [8192, 8192], P('ctx', 'tp'), may hold values from -6 to 6
- prefix_z: bfloat16 [8192, 8192], P('ctx', 'tp'), may hold values from -6 to 6
- prefix_bc: bfloat16 [8192, 256], P(('ctx', 'tp')), may hold values from -6 to 6
- prefix_dt: float32 [128, 8192], P('tp', 'ctx'), may hold values from -6 to 6
- branch_x: bfloat16 [8192, 8192], P('ctx', 'tp'), may hold values from -6 to 6
- branch_z: bfloat16 [8192, 8192], P('ctx', 'tp'), may hold values from -6 to 6
- branch_bc: bfloat16 [8192, 256], P(('ctx', 'tp')), may hold values from -6 to 6
- branch_dt: float32 [128, 8192], P('tp', 'ctx'), may hold values from -6 to 6
- conv_x: bfloat16 [4, 8192], P(None, 'tp'), may hold values from -3 to 3
- conv_bc: bfloat16 [4, 256], replicated, may hold values from -3 to 3
- decay_rate: float32 [128], P('tp'), may hold values from 2.4414063e-05 to 0.03
- skip: float32 [128], P('tp'), may hold values from 0.5 to 1.5
- norm_gain: float32 [8192], P('tp'), may hold values from 0.5 to 1.5
- bound_pos: int32 [8], replicated, may hold values from 0 to 8191
- branch_owner: int32 [64], replicated, may hold values from 0 to 31, as said below
- branch_parent: int32 [64], replicated, may hold values from 0 to 7
- branch_len: int32 [64], replicated, may hold values from 1 to 255, as said below
Outputs:
- prefix_out: bfloat16 [8192, 8192], P('ctx', 'tp')
- branch_out: bfloat16 [8192, 8192], P('ctx', 'tp')
Inputs may be any that keep to these rules, and one draw needn't show every extreme that they name: `branch_owner`: every block index 0 to 31 holds exactly 2 branches. `branch_len`: the branches of one block have lengths that sum to at most 256; in every draw some block's sum is exactly 256, and some branch has exactly 255 rows.
All inputs are finite; a program needn't handle non-finite values.
Results may differ from a plain program's by a relative error of at most 0.0034.
Values may be sent and summed in bfloat16 or wider, within the bound.
No kernel may reach another device: no remote copies, remote signals or barrier semaphores. Data moves between devices by JAX's collectives and lax.ppermute only.
A program may use at most 64 MiB of HBM per device.

v0:
```python
import jax
import jax.numpy as jnp
from jax import lax
from jax.sharding import PartitionSpec as P

BR_PER = 2
EPSILON = 1e-05
SLOTS = 8
BF = jnp.bfloat16
F32 = jnp.float32
HIGH = lax.Precision.HIGHEST


def conv_silu(lagged, weights):
    summed = weights[0].astype(F32)[None, :] * lagged[0].astype(F32)
    for tap in range(1, len(lagged)):
        summed = summed + weights[tap].astype(F32)[None, :] * lagged[tap].astype(F32)
    return jax.nn.silu(summed).astype(BF)


def split_conv(convolved, channels, heads):
    length = convolved.shape[0]
    state = (convolved.shape[1] - channels) // 2
    values = convolved[:, :channels].reshape(length, heads, channels // heads)
    return (values, convolved[:, channels : channels + state], convolved[:, channels + state :])


def decays(raw_steps, rates):
    length = raw_steps.shape[1]
    step = jax.nn.softplus(raw_steps)
    log_decay = -rates[:, None] * step
    index = jnp.arange(length, dtype=jnp.int32)
    upper = (index[:, None] <= index[None, :]).astype(F32)
    return (step, log_decay, jnp.dot(log_decay, upper, precision=HIGH))


def intra(values, b_rows, c_rows, step, cumulative, mask):
    scores = jnp.dot(c_rows, b_rows.T, preferred_element_type=F32)
    exponent = jnp.where(mask[None], cumulative[:, :, None] - cumulative[:, None, :], 0.0)
    mixing = jnp.where(mask[None], scores[None] * jnp.exp(exponent) * step[:, None, :], 0.0)
    return jnp.einsum("hts,shp->thp", mixing.astype(BF), values, preferred_element_type=F32)


def pick(array, positions):
    index = jnp.arange(array.shape[1], dtype=jnp.int32)
    hit = index[None, None, :] == positions[:, None, None]
    return jnp.sum(jnp.where(hit, array[None], 0.0), axis=2)


def local_states(values, b_rows, step, cumulative, positions):
    length = cumulative.shape[1]
    ends = pick(cumulative, positions)
    row = jnp.arange(length, dtype=jnp.int32)
    inside = (row[None, :] <= positions[:, None])[:, None, :]
    exponent = jnp.where(inside, ends[:, :, None] - cumulative[None], 0.0)
    weight = jnp.where(inside, jnp.exp(exponent) * step[None], 0.0)
    weighted = (jnp.transpose(weight, (0, 2, 1))[:, :, :, None] * values[None].astype(F32)).astype(
        BF
    )
    states = jnp.einsum("jshp,sn->jhpn", weighted, b_rows, preferred_element_type=F32)
    return (states, ends)


def from_state(c_rows, state, weight):
    result = jnp.einsum("tn,hpn->thp", c_rows, state, preferred_element_type=F32)
    return result * weight.T[:, :, None]


def parts_of(value, count):
    found = []
    for _ in range(count):
        part = lax.reduce_precision(value, 8, 7)
        found.append(part.astype(BF))
        value = value - part
    return found


def body(
    prefix_x,
    prefix_z,
    prefix_bc,
    prefix_dt,
    branch_x,
    branch_z,
    branch_bc,
    branch_dt,
    conv_x,
    conv_bc,
    decay_rate,
    skip,
    norm_gain,
    bound_pos,
    branch_owner,
    branch_parent,
    branch_len,
):
    n_ctx = lax.axis_size("ctx")
    me = lax.axis_index("ctx")
    length, channels = prefix_x.shape
    heads = decay_rate.shape[0]
    width = prefix_bc.shape[1]
    n_state = width // 2
    bounds = bound_pos.shape[0]
    branches = branch_owner.shape[0]
    weights = jnp.concatenate([conv_x, conv_bc], axis=1)
    taps = weights.shape[0]
    tail = taps - 1
    row_width = channels + width
    gathered = lax.all_gather(
        jnp.concatenate([prefix_bc, branch_bc], axis=1), "tp", axis=0, tiled=True
    )
    joined = jnp.concatenate([prefix_x, gathered[:, :width]], axis=1)
    before = lax.ppermute(joined[length - tail :], "ctx", [(i, i + 1) for i in range(n_ctx - 1)])
    extended = jnp.concatenate([before, joined], axis=0)
    lagged = [extended[tap : tap + length] for tap in range(taps)]
    values, b_rows, c_rows = split_conv(conv_silu(lagged, weights), channels, heads)
    step, _, cumulative = decays(prefix_dt, decay_rate)
    block_of = bound_pos // length
    at = bound_pos - block_of * length
    order = jnp.arange(bounds, dtype=jnp.int32)
    slot_of = jnp.sum(
        ((block_of[:, None] == block_of[None, :]) & (order[None, :] < order[:, None])).astype(
            jnp.int32
        ),
        axis=1,
    )
    border = jnp.arange(branches, dtype=jnp.int32)
    same = branch_owner[:, None] == branch_owner[None, :]
    earlier = same & (border[None, :] < border[:, None])
    rank = jnp.sum(earlier.astype(jnp.int32), axis=1)
    start = jnp.sum(jnp.where(earlier, branch_len[None, :], 0), axis=1)
    place = jnp.arange(n_ctx * BR_PER, dtype=jnp.int32)
    chosen = place[:, None] == (branch_owner * BR_PER + rank)[None, :]
    parent_of = jnp.sum(jnp.where(chosen, branch_parent[None, :], 0), axis=1)
    mine = (me * BR_PER + jnp.arange(BR_PER, dtype=jnp.int32))[:, None] == (
        branch_owner * BR_PER + rank
    )[None, :]
    my_len = jnp.sum(jnp.where(mine, branch_len[None, :], 0), axis=1)
    my_start = jnp.sum(jnp.where(mine, start[None, :], 0), axis=1)
    slot_here = (block_of == me)[None, :] & (
        slot_of[None, :] == jnp.arange(SLOTS, dtype=jnp.int32)[:, None]
    )
    positions = jnp.sum(jnp.where(slot_here, at[None, :] + 1, 0), axis=1) - 1
    positions = jnp.concatenate([jnp.full((1,), length - 1, jnp.int32), positions])
    states, ends = local_states(values, b_rows, step, cumulative, positions)
    slices = states.reshape(SLOTS + 1, n_ctx, -1, n_state)
    rows = slices.shape[2]
    end_hi, end_lo = parts_of(slices[0], 2)
    partial = jnp.transpose(slices[1:].astype(BF), (1, 0, 2, 3)).reshape(
        n_ctx, SLOTS * rows, n_state
    )
    per_head = jnp.repeat(
        jnp.pad(ends.T, ((0, 0), (0, n_state - SLOTS - 1))), n_ctx // heads, axis=0
    )
    logs = jnp.stack(parts_of(per_head, 3), axis=1)
    parent_hit = parent_of[:, None] == order[None, :]
    parent_at = jnp.sum(jnp.where(parent_hit, at[None, :], 0), axis=1)
    parent_block = jnp.sum(jnp.where(parent_hit, block_of[None, :], 0), axis=1)
    wanted = parent_at[:, None] + 1 + jnp.arange(tail, dtype=jnp.int32)[None, :]
    wanted = jnp.where((parent_block == me)[:, None], wanted, -1).reshape(-1)
    picker = (wanted[:, None] == jnp.arange(length + tail, dtype=jnp.int32)[None, :]).astype(BF)
    tails = jnp.dot(picker, extended, preferred_element_type=F32).astype(BF)
    tails = tails.reshape(n_ctx, BR_PER * tail * row_width // n_state, n_state)
    pieces = [end_hi, end_lo, partial, tails, logs]
    sent = jnp.concatenate(pieces, axis=1)
    sent = jnp.pad(sent, ((0, 0), (0, -sent.shape[1] % 16), (0, 0)))
    got = lax.all_to_all(sent, "ctx", 0, 0, tiled=True)
    edges = [0]
    for piece in pieces:
        edges.append(edges[-1] + piece.shape[1])
    end_hi, end_lo, partial, tails, logs = [
        got[:, first:last].astype(F32) for first, last in zip(edges[:-1], edges[1:], strict=True)
    ]
    ends = jnp.sum(logs, axis=1)[:, : SLOTS + 1]
    block = jnp.arange(n_ctx, dtype=jnp.int32)
    totals = jnp.sum(jnp.where(block[None, :] <= block[:, None], ends[:, 0][None, :], 0.0), axis=1)
    gap = (totals - ends[:, 0])[:, None] - totals[None, :]
    earlier_block = block[None, :] < block[:, None]
    carry = jnp.where(earlier_block, jnp.exp(jnp.where(earlier_block, gap, 0.0)), 0.0)
    entering = jnp.dot(carry, (end_hi + end_lo).reshape(n_ctx, -1), precision=HIGH)
    held = block[None, :] == block_of[:, None]
    bound_end = jnp.sum(
        jnp.where(
            held[:, :, None]
            & (slot_of[:, None, None] == jnp.arange(SLOTS, dtype=jnp.int32)[None, None, :]),
            ends[None, :, 1:],
            0.0,
        ),
        axis=(1, 2),
    )
    choose = jnp.where(held, jnp.exp(bound_end)[:, None], 0.0)
    slot_pick = (
        held[:, :, None]
        & (slot_of[:, None, None] == jnp.arange(SLOTS, dtype=jnp.int32)[None, None, :])
    ).reshape(bounds, -1)
    bound_state = jnp.dot(choose, entering, precision=HIGH) + jnp.dot(
        slot_pick.astype(BF),
        partial.astype(BF).reshape(n_ctx * SLOTS, -1),
        preferred_element_type=F32,
    )
    seeds = jnp.dot(parent_hit.astype(F32), bound_state, precision=HIGH).reshape(
        n_ctx, BR_PER * rows, n_state
    )
    back = jnp.concatenate([entering.reshape(n_ctx, rows, n_state), seeds], axis=1).astype(BF)
    back = lax.all_to_all(back, "ctx", 0, 0, tiled=True)
    row = jnp.arange(length, dtype=jnp.int32)
    mixed = intra(values, b_rows, c_rows, step, cumulative, row[None, :] <= row[:, None])
    inside = (row[None, :] >= my_start[:, None]) & (row[None, :] < (my_start + my_len)[:, None])
    live = inside[0] | inside[1]
    segment = jnp.where(inside[0], 0, jnp.where(inside[1], 1, BR_PER))
    offset = row - jnp.sum(jnp.where(inside, my_start[:, None], 0), axis=0)
    tail_rows = jnp.sum(tails, axis=0).astype(BF).reshape(BR_PER * tail, row_width)
    branch_joined = jnp.concatenate([branch_x, gathered[:, width:]], axis=1)
    column = jnp.arange(BR_PER * tail, dtype=jnp.int32)
    lagged = []
    for shift in range(tail, 0, -1):
        shifted = jnp.concatenate(
            [jnp.zeros((shift, row_width), BF), branch_joined[: length - shift]], axis=0
        )
        local = jnp.where((offset >= shift)[:, None], shifted, jnp.zeros_like(shifted))
        picker = (
            (segment[:, None] == (column // tail)[None, :])
            & (offset[:, None] < shift)
            & ((column % tail)[None, :] == tail - shift + offset[:, None])
        ).astype(BF)
        lagged.append(local + jnp.dot(picker, tail_rows, preferred_element_type=F32).astype(BF))
    lagged.append(branch_joined)
    b_values, b_b, b_c = split_conv(conv_silu(lagged, weights), channels, heads)
    b_step, b_log, b_cum = decays(branch_dt, decay_rate)
    mask = (segment[:, None] == segment[None, :]) & live[:, None] & (row[None, :] <= row[:, None])
    b_mixed = intra(b_values, b_b, b_c, b_step, b_cum, mask)
    starts = pick(b_cum - b_log, my_start)
    gap = b_cum - jnp.where(inside[0][None, :], starts[0][:, None], starts[1][:, None])
    seed_weight = jnp.where(live[None, :], jnp.exp(jnp.where(live[None, :], gap, 0.0)), 0.0)
    shape = (heads, channels // heads, n_state)
    mixed = mixed + from_state(c_rows, back[:, :rows].reshape(shape), jnp.exp(cumulative))
    for slot in range(BR_PER):
        seed = back[:, (slot + 1) * rows : (slot + 2) * rows].reshape(shape)
        b_mixed = b_mixed + from_state(
            b_c, seed, jnp.where(inside[slot][None, :], seed_weight, 0.0)
        )

    def gate(mixed, values, z):
        mixed = mixed + skip[None, :, None] * values.astype(F32)
        gated = mixed.reshape(length, -1) * jax.nn.silu(z.astype(F32))
        return (gated, jnp.sum(gated * gated, axis=1))

    gated, squares = gate(mixed, values, prefix_z)
    b_gated, b_squares = gate(b_mixed, b_values, branch_z)
    every = lax.all_gather(jnp.stack([squares, b_squares])[None], "tp", axis=0, tiled=True)
    factor = lax.rsqrt(jnp.sum(every, axis=0) / (channels * lax.axis_size("tp")) + EPSILON)
    prefix_out = (gated * factor[0][:, None] * norm_gain[None, :]).astype(BF)
    branch_out = (b_gated * factor[1][:, None] * norm_gain[None, :]).astype(BF)
    return (prefix_out, jnp.where(live[:, None], branch_out, jnp.zeros_like(branch_out)))


def solution(mesh):
    both = P(("ctx", "tp"), None)
    in_specs = (
        P("ctx", "tp"),
        P("ctx", "tp"),
        both,
        P("tp", "ctx"),
        P("ctx", "tp"),
        P("ctx", "tp"),
        both,
        P("tp", "ctx"),
        P(None, "tp"),
        P(),
        P("tp"),
        P("tp"),
        P("tp"),
        P(),
        P(),
        P(),
        P(),
    )
    out_specs = (P("ctx", "tp"), P("ctx", "tp"))
    return jax.shard_map(body, mesh=mesh, in_specs=in_specs, out_specs=out_specs, check_vma=False)
```

profile of v0, /device:TPU:1, one launch (start us, length us, event | category | flops | bytes accessed | tf_op | source)
XLA Modules:
  0.0 158.5 jit_solution(17156961118969503318)
XLA Ops:
  1.4 25.2 %all_gather.6 = bf16[256,512]{1,0:T(8,128)(2,1)S(1)} all-gather(bf16[16,512]{1,0:T(8,128)(2,1)S(1)} %pad_maximum_fusion.3), channel_id=1, replica_groups=mesh['ctx'=32,'tp'=16] {'tp'}, dimensions={0}, use_global_device_ids=true | all-gather | bytes 278528 | tf_op jit(solution)/shard_map/all_gather | solution.py:109
  27.3 3.2 %collective-permute-start = (bf16[3,768]{1,0:T(4,128)(2,1)S(1)}, bf16[3,768]{1,0:T(4,128)(2,1)S(1)}, u32[]{:S(2)}, u32[]{:S(2)}) collective-permute-start(bf16[3,768]{1,0:T(4,128)(2,1)S(1)} %fusion.90), channel_id=1, source_target_pairs={{0,16},{16,32},{32,48},{48,64},{64,80},{80,96},{96,112},{112,128},... | collective-permute-start | bytes 13832 | tf_op jit(solution)/shard_map/ppermute | solution.py:113
  33.1 1.3 compare_select_fusion.1
  34.4 1.5 bitcast_exponential_fusion
  36.7 1.4 select_reduce_fusion.2
  43.1 1.0 maximum_maximum_fusion
  47.7 3.7 %concatenate.39 = bf16[32,199,128]{2,1,0:T(8,128)(2,1)S(1)} concatenate(bf16[32,16,128]{2,1,0:T(8,128)(2,1)} %get-tuple-element.25, bf16[32,16,128]{2,1,0:T(8,128)(2,1)} %get-tuple-element.24, bf16[32,128,128]{2,1,0:T(8,128)(2,1)S(1)} %bitcast.88, bf16[32,36,128]{2,1,0:T(8,128)(2,1)S(1)} %reshape.471, bf16[32,1,128]{2,1,0:T(2,128)(2,1)S(1)} %copy.56, bf16[32,1,128]{2,1,0:T(2,128)(2,1)} %copy.57, ...), dimensions={1} | concatenate | bytes 3260416 | tf_op jit(solution)/shard_map/concatenate | solution.py:165
  51.4 1.3 pad.12
  52.7 8.9 %all-to-all-start = ((bf16[32,208,128]{2,1,0:T(8,128)(2,1)}), bf16[32,208,128]{2,1,0:T(8,128)(2,1)S(1)}, u32[]{:S(2)}, u32[]{:S(2)}) async-start(bf16[32,208,128]{2,1,0:T(8,128)(2,1)} %pad.12), calls=%async_computation | async-start | bytes 3407872 | tf_op jit(solution)/shard_map/all_to_all | solution.py:167
  65.5 0.8 fusion.42
  69.7 0.9 fusion.59
  70.6 31.0 %all-to-all-done = bf16[32,208,128]{2,1,0:T(8,128)(2,1)S(1)} async-done(((bf16[32,208,128]{2,1,0:T(8,128)(2,1)}), bf16[32,208,128]{2,1,0:T(8,128)(2,1)S(1)}, u32[]{:S(2)}, u32[]{:S(2)}) %all-to-all-start) | async-done | bytes 1703968 | tf_op jit(solution)/shard_map/all_to_all | solution.py:167
  103.0 1.1 slice.184
  104.1 1.5 reshape.475
  105.7 1.4 select_reduce_fusion.5
  107.0 1.4 copy.59
  108.4 0.8 subtract_reduce_fusion
  109.2 0.9 select_reduce_fusion
  110.2 1.1 fusion.46
  112.0 0.9 fusion.99
  112.9 0.9 convolution_add_fusion
  114.4 0.9 copy.66
  116.1 7.5 %all-to-all-start.1 = ((bf16[32,48,128]{2,1,0:T(8,128)(2,1)}), bf16[32,48,128]{2,1,0:T(8,128)(2,1)S(1)}, u32[]{:S(2)}, u32[]{:S(2)}) async-start(bf16[32,48,128]{2,1,0:T(8,128)(2,1)} %pad_maximum_fusion.2), calls=%async_computation.1 | async-start | bytes 786432 | tf_op jit(solution)/shard_map/all_to_all | solution.py:205
  123.7 1.5 fusion.16
  125.2 1.1 fusion.19
  127.2 0.8 copy.61
  128.0 0.9 fusion.52
  128.9 5.3 %all-to-all-done.1 = bf16[32,48,128]{2,1,0:T(8,128)(2,1)S(1)} async-done(((bf16[32,48,128]{2,1,0:T(8,128)(2,1)}), bf16[32,48,128]{2,1,0:T(8,128)(2,1)S(1)}, u32[]{:S(2)}, u32[]{:S(2)}) %all-to-all-start.1) | async-done | bytes 393248 | tf_op jit(solution)/shard_map/all_to_all | solution.py:205
  136.4 0.8 fusion.7
  137.9 18.7 %all-gather.1 = f32[16,2,256]{2,1,0:T(2,128)S(1)} all-gather(f32[1,2,256]{2,1,0:T(2,128)S(1)} %maximum_bitcast_fusion), channel_id=2, replica_groups=mesh['ctx'=32,'tp'=16] {'tp'}, dimensions={0}, use_global_device_ids=true | all-gather | bytes 34816 | tf_op jit(solution)/shard_map/all_gather | solution.py:250
  156.7 0.9 fusion.45
  157.6 0.9 multiply_convert_fusion.5
  (200 shorter events, 27.4 us)
Async XLA Ops:
  0.6 43.6 %copy-start.1 = (bf16[256,512]{1,0:T(8,128)(2,1)S(1)}, bf16[256,512]{1,0:T(8,128)(2,1)}, u32[]{:S(2)}) copy-start(bf16[256,512]{1,0:T(8,128)(2,1)} %param.17) | copy-start | bytes 786436
  27.3 15.8 %collective-permute-start = (bf16[3,768]{1,0:T(4,128)(2,1)S(1)}, bf16[3,768]{1,0:T(4,128)(2,1)S(1)}, u32[]{:S(2)}, u32[]{:S(2)}) collective-permute-start(bf16[3,768]{1,0:T(4,128)(2,1)S(1)} %fusion.90), channel_id=1, source_target_pairs={{0,16},{16,32},{32,48},{48,64},{64,80},{80,96},{96,112},{112,128},... | collective-permute-start | bytes 13832 | tf_op jit(solution)/shard_map/ppermute | solution.py:113
  31.2 8.6 %copy-start.30 = (s32[8]{0:T(128)}, s32[8]{0:T(128)S(1)}, u32[]{:S(2)}) copy-start(s32[8]{0:T(128)S(1)} %get-tuple-element.16) | copy-start | bytes 100
  32.1 12.1 %copy-start.34 = (pred[8,32]{1,0:T(8,128)(4,1)}, pred[8,32]{1,0:T(8,128)(4,1)S(1)}, u32[]{:S(2)}) copy-start(pred[8,32]{1,0:T(8,128)(4,1)S(1)} %iota_compare_fusion.14) | copy-start | bytes 772
  32.2 12.0 %copy-start.35 = (pred[8,8]{1,0:T(8,128)(4,1)}, pred[8,8]{1,0:T(8,128)(4,1)S(1)}, u32[]{:S(2)}) copy-start(pred[8,8]{1,0:T(8,128)(4,1)S(1)} %iota_compare_fusion.13) | copy-start | bytes 196
  36.0 8.7 %copy-start.20 = (f32[8,256]{1,0:T(8,128)}, f32[8,256]{1,0:T(8,128)S(1)}, u32[]{:S(2)}) copy-start(f32[8,256]{1,0:T(8,128)S(1)} %get-tuple-element.54) | copy-start | bytes 24580
  52.7 9.0 %copy-start.11 = (pred[8,32,8]{2,1,0:T(8,128)(4,1)S(1)}, pred[8,32,8]{2,1,0:T(8,128)(4,1)}, u32[]{:S(2)}) copy-start(pred[8,32,8]{2,1,0:T(8,128)(4,1)} %broadcast_and_fusion) | copy-start | bytes 6148
  52.7 9.7 %copy-start.42 = (s32[64]{0:T(128)S(1)}, s32[64]{0:T(128)}, u32[]{:S(2)}) copy-start(s32[64]{0:T(128)} %param.33) | copy-start | bytes 772
  52.7 9.7 %copy-start.43 = (s32[64]{0:T(128)S(1)}, s32[64]{0:T(128)}, u32[]{:S(2)}) copy-start(s32[64]{0:T(128)} %get-tuple-element.11) | copy-start | bytes 772
  52.7 9.7 %copy-start.46 = (s32[64]{0:T(128)S(1)}, s32[64]{0:T(128)}, u32[]{:S(2)}) copy-start(s32[64]{0:T(128)} %copy-done.45) | copy-start | bytes 772
  52.7 10.6 %copy-start.49 = (f32[8,256]{1,0:T(8,128)S(1)}, f32[8,256]{1,0:T(8,128)}, u32[]{:S(2)}) copy-start(f32[8,256]{1,0:T(8,128)} %param.24) | copy-start | bytes 24580
  52.7 10.6 %copy-start.52 = (f32[8]{0:T(128)S(1)}, f32[8]{0:T(128)}, u32[]{:S(2)}) copy-start(f32[8]{0:T(128)} %copy-done.51) | copy-start | bytes 100
  52.7 12.0 %copy-start = (bf16[256,512]{1,0:T(8,128)(2,1)S(1)}, bf16[256,512]{1,0:T(8,128)(2,1)}, u32[]{:S(2)}) copy-start(bf16[256,512]{1,0:T(8,128)(2,1)} %param.21) | copy-start | bytes 786436
  52.7 48.9 %all-to-all-start = ((bf16[32,208,128]{2,1,0:T(8,128)(2,1)}), bf16[32,208,128]{2,1,0:T(8,128)(2,1)S(1)}, u32[]{:S(2)}, u32[]{:S(2)}) async-start(bf16[32,208,128]{2,1,0:T(8,128)(2,1)} %pad.12), calls=%async_computation | async-start | bytes 3407872 | tf_op jit(solution)/shard_map/all_to_all | solution.py:167
  62.7 40.3 %copy-start.36 = (pred[256]{0:T(512)(128)(4,1)}, pred[256]{0:T(512)(128)(4,1)S(1)}, u32[]{:S(2)}) copy-start(pred[256]{0:T(512)(128)(4,1)S(1)} %or.10) | copy-start | bytes 772
  64.0 39.1 %copy-start.32 = (f32[8,256]{1,0:T(8,128)}, f32[8,256]{1,0:T(8,128)S(1)}, u32[]{:S(2)}) copy-start(f32[8,256]{1,0:T(8,128)S(1)} %get-tuple-element.52) | copy-start | bytes 24580
  67.1 35.9 %copy-start.22 = (s32[256]{0:T(256)}, s32[256]{0:T(256)S(1)}, u32[]{:S(2)}) copy-start(s32[256]{0:T(256)S(1)} %select_select_fusion.1) | copy-start | bytes 3076
  112.9 10.8 %copy-start.17 = (f32[768]{0:T(1024)S(1)}, f32[768]{0:T(1024)}, u32[]{:S(2)}) copy-start(f32[768]{0:T(1024)} %copy-done.16) | copy-start | bytes 9220
  112.9 10.8 %copy-start.23 = (s32[256]{0:T(256)S(1)}, s32[256]{0:T(256)}, u32[]{:S(2)}) copy-start(s32[256]{0:T(256)} %copy-done.22) | copy-start | bytes 3076
  113.8 11.4 %copy-start.2 = (bf16[255,768]{1,0:T(8,128)(2,1)S(1)}, bf16[255,768]{1,0:T(8,128)(2,1)}, u32[]{:S(2)}) copy-start(bf16[255,768]{1,0:T(8,128)(2,1)} %fusion.42) | copy-start | bytes 1175044
  113.8 11.4 %copy-start.15 = (f32[768]{0:T(1024)S(1)}, f32[768]{0:T(1024)}, u32[]{:S(2)}) copy-start(f32[768]{0:T(1024)} %copy-done.14) | copy-start | bytes 9220
  115.3 11.0 %copy-start.25 = (f32[768]{0:T(1024)S(1)}, f32[768]{0:T(1024)}, u32[]{:S(2)}) copy-start(f32[768]{0:T(1024)} %copy-done.24) | copy-start | bytes 9220
  116.1 10.2 %copy-start.27 = (f32[768]{0:T(1024)S(1)}, f32[768]{0:T(1024)}, u32[]{:S(2)}) copy-start(f32[768]{0:T(1024)} %copy-done.26) | copy-start | bytes 9220
  116.1 10.2 %copy-start.38 = (s32[6]{0:T(128)S(1)}, s32[6]{0:T(128)}, u32[]{:S(2)}) copy-start(s32[6]{0:T(128)} %get-tuple-element.55) | copy-start | bytes 76
  116.1 10.2 %copy-start.39 = (s32[6]{0:T(128)S(1)}, s32[6]{0:T(128)}, u32[]{:S(2)}) copy-start(s32[6]{0:T(128)} %get-tuple-element.56) | copy-start | bytes 76
  116.1 10.2 %copy-start.44 = (s32[256]{0:T(256)S(1)}, s32[256]{0:T(256)}, u32[]{:S(2)}) copy-start(s32[256]{0:T(256)} %get-tuple-element.43) | copy-start | bytes 3076
  116.1 10.2 %copy-start.47 = (pred[256]{0:T(512)(128)(4,1)S(1)}, pred[256]{0:T(512)(128)(4,1)}, u32[]{:S(2)}) copy-start(pred[256]{0:T(512)(128)(4,1)} %get-tuple-element.37) | copy-start | bytes 772
  116.1 10.2 %copy-start.48 = (pred[256]{0:T(512)(128)(4,1)S(1)}, pred[256]{0:T(512)(128)(4,1)}, u32[]{:S(2)}) copy-start(pred[256]{0:T(512)(128)(4,1)} %get-tuple-element.38) | copy-start | bytes 772
  116.1 18.0 %all-to-all-start.1 = ((bf16[32,48,128]{2,1,0:T(8,128)(2,1)}), bf16[32,48,128]{2,1,0:T(8,128)(2,1)S(1)}, u32[]{:S(2)}, u32[]{:S(2)}) async-start(bf16[32,48,128]{2,1,0:T(8,128)(2,1)} %pad_maximum_fusion.2), calls=%async_computation.1 | async-start | bytes 786432 | tf_op jit(solution)/shard_map/all_to_all | solution.py:205
  127.1 7.4 %copy-start.6 = (bf16[256,512]{0,1:T(8,128)(2,1)S(1)}, bf16[256,512]{0,1:T(8,128)(2,1)}, u32[]{:S(2)}) copy-start(bf16[256,512]{0,1:T(8,128)(2,1)} %copy-done.5) | copy-start | bytes 786436
  137.2 19.5 %copy-start.29 = (f32[512]{0:T(512)S(1)}, f32[512]{0:T(512)}, u32[]{:S(2)}) copy-start(f32[512]{0:T(512)} %param.29) | copy-start | bytes 6148
  137.2 19.5 %copy-start.37 = (pred[256]{0:T(512)(128)(4,1)S(1)}, pred[256]{0:T(512)(128)(4,1)}, u32[]{:S(2)}) copy-start(pred[256]{0:T(512)(128)(4,1)} %copy-done.36) | copy-start | bytes 772
  (25 other events, 78.7 us)
where the time goes:
time: 160 us; the launch traced here: 158 us
  blocking collectives  43.9 us (27%)
  waiting for transfers between devices  36.3 us (23%)
  other arithmetic  25.4 us (16%)
  starting transfers between devices  19.6 us (12%)
  local copies, waits for them, and re-layouts  17.9 us (11%)
  matrix products  13.9 us (9%)
    all_to_all x1, waiting for transfers between devices, body(): got = lax.all_to_all(sent, 'ctx', 0, 0, tiled=True)  31 us
    all_gather x1, blocking collectives, body(): lax.all_gather(jnp.concatenate([prefix_bc, branch_bc], axis=1), 'tp', axi...  25.2 us
    all_gather x1, blocking collectives, body(): lax.all_gather(jnp.stack([squares, b_squares])[None], 'tp', axis=0, tiled...  18.7 us
    all_to_all x1, starting transfers between devices, body(): got = lax.all_to_all(sent, 'ctx', 0, 0, tiled=True)  8.92 us
    all_to_all x1, starting transfers between devices, body(): back = lax.all_to_all(back, 'ctx', 0, 0, tiled=True)  7.45 us
    all_to_all x1, waiting for transfers between devices, body(): back = lax.all_to_all(back, 'ctx', 0, 0, tiled=True)  5.25 us
    concatenate x1, local copies, waits for them, and re-layouts, body(): sent = jnp.concatenate(pieces, axis=1)  3.65 us
    dot_general x3, matrix products, body(): jnp.dot(picker, tail_rows, preferred_element_type=F32).astype(BF)  3.24 us
  transfers between devices with their start and end apart: 3, of which 2 were waited for; matrix products, arithmetic and copies ran while one was open for 17% of the time, Pallas kernels for 0%

commit v1 on v0

--- a/solution.py
+++ b/solution.py
@@ -106,8 +106,14 @@
     taps = weights.shape[0]
     tail = taps - 1
     row_width = channels + width
-    gathered = lax.all_gather(
-        jnp.concatenate([prefix_bc, branch_bc], axis=1), "tp", axis=0, tiled=True
+    gathered = jnp.concatenate(
+        lax.all_to_all(
+            jnp.stack([jnp.concatenate([prefix_bc, branch_bc], axis=1)] * lax.axis_size("tp")),
+            "tp",
+            0,
+            0,
+        ),
+        axis=0,
     )
     joined = jnp.concatenate([prefix_x, gathered[:, :width]], axis=1)
     before = lax.ppermute(joined[length - tail :], "ctx", [(i, i + 1) for i in range(n_ctx - 1)])

time: 160 us -> 148 us (0.925)
  blocking collectives: 43.9 us -> 20.4 us
  starting transfers between devices: 19.6 us -> 34.3 us
  matrix products: 13.9 us -> 17.2 us
  other arithmetic: 25.4 us -> 23.2 us
  local copies, waits for them, and re-layouts: 17.9 us -> 15.8 us
    all_gather x1 -> x0, blocking collectives: 25.2 us -> none  [body(): lax.all_gather(jnp.concatenate([prefix_bc, branch_bc], axis=1), 'tp', axi...]
    all_to_all x0 -> x1, starting transfers between devices: none -> 11.8 us  [body(): lax.all_to_all(jnp.stack([jnp.concatenate([prefix_bc, branch_bc], axis=1)...]
    all_to_all x1, starting transfers between devices: 8.92 us -> 11.8 us  [body(): got = lax.all_to_all(sent, 'ctx', 0, 0, tiled=True)]
    all_to_all x1, waiting for transfers between devices: 5.25 us -> 2.65 us  [body(): back = lax.all_to_all(back, 'ctx', 0, 0, tiled=True)]
    concatenate x1, local copies, waits for them, and re-layouts: 3.65 us -> 1.13 us  [body(): sent = jnp.concatenate(pieces, axis=1)]
    all_gather x1, blocking collectives: 18.7 us -> 20.4 us  [body(): lax.all_gather(jnp.stack([squares, b_squares])[None], 'tp', axis=0, tiled...]
    dot_general x3, matrix products: 0.67 us -> 2.34 us  [from_state(): jnp.einsum('tn,hpn->thp', c_rows, state, preferred_element_type=F32)]
  transfers between devices with their start and end apart: 3 -> 4, of which waited for: 2 -> 4; matrix products, arithmetic and copies ran while one was open for 17% -> 18% of each run, Pallas kernels for 0% -> 0%
where the time goes in v1:
time: 148 us; the launch traced here: 147 us
  waiting for transfers between devices  34.9 us (24%)
  starting transfers between devices  34.3 us (23%)
  other arithmetic  23.2 us (16%)
  blocking collectives  20.4 us (14%)
  matrix products  17.2 us (12%)
  local copies, waits for them, and re-layouts  15.8 us (11%)
  between operations  1.59 us (1%)
    all_to_all x1, waiting for transfers between devices, body(): got = lax.all_to_all(sent, 'ctx', 0, 0, tiled=True)  30.9 us
    all_gather x1, blocking collectives, body(): lax.all_gather(jnp.stack([squares, b_squares])[None], 'tp', axis=0, tiled...  20.4 us
    all_to_all x1, starting transfers between devices, body(): lax.all_to_all(jnp.stack([jnp.concatenate([prefix_bc, branch_bc], axis=1)...  11.8 us
    all_to_all x1, starting transfers between devices, body(): got = lax.all_to_all(sent, 'ctx', 0, 0, tiled=True)  11.8 us
    all_to_all x1, starting transfers between devices, body(): back = lax.all_to_all(back, 'ctx', 0, 0, tiled=True)  7.47 us
    dot_general x3, matrix products, body(): jnp.dot(picker, tail_rows, preferred_element_type=F32).astype(BF)  4.01 us
    ppermute x1, starting transfers between devices, body(): lax.ppermute(joined[length - tail:], 'ctx', [(i, i + 1) for i in range(n_...  3.2 us
  transfers between devices with their start and end apart: 4, of which 4 were waited for; matrix products, arithmetic and copies ran while one was open for 18% of the time, Pallas kernels for 0%

profile of v1, /device:TPU:1, one launch (start us, length us, event | category | flops | bytes accessed | tf_op | source)
XLA Modules:
  0.0 147.3 jit_solution(5981731337357208059)
XLA Ops:
  2.1 11.8 %all-to-all-start = ((bf16[16,16,512]{2,1,0:T(8,128)(2,1)}), bf16[16,16,512]{2,1,0:T(8,128)(2,1)S(1)}, u32[]{:S(2)}, u32[]{:S(2)}) async-start(bf16[16,16,512]{2,1,0:T(8,128)(2,1)} %stack.8), calls=%async_computation | async-start | bytes 524288 | tf_op jit(solution)/shard_map/all_to_all | solution.py:110
  16.6 1.3 compare_select_fusion.1
  17.9 1.5 %bitcast_exponential_fusion = (f32[256,8]{0,1:T(8,128)}, f32[8,256]{1,0:T(8,128)S(1)}) fusion(f32[8]{0:T(128)S(1)} %neg.27, f32[8,256]{1,0:T(8,128)} %param.20), kind=kOutput, calls=%fused_computation.253 | convolution fusion | flops 6371328 | bytes 24608 | tf_op jit(solution)/shard_map/dot_general | solution.py:34
  20.1 0.9 select_reduce_fusion.2
  26.4 3.2 %collective-permute-start = (bf16[3,768]{1,0:T(4,128)(2,1)S(1)}, bf16[3,768]{1,0:T(4,128)(2,1)S(1)}, u32[]{:S(2)}, u32[]{:S(2)}) collective-permute-start(bf16[3,768]{1,0:T(4,128)(2,1)S(1)} %fusion.90), channel_id=1, source_target_pairs={{0,16},{16,32},{32,48},{48,64},{64,80},{80,96},{96,112},{112,128},... | collective-permute-start | bytes 13832 | tf_op jit(solution)/shard_map/ppermute | solution.py:119
  33.3 1.1 concatenate.39
  34.4 1.3 pad.12
  35.8 11.8 %all-to-all-start.1 = ((bf16[32,208,128]{2,1,0:T(8,128)(2,1)}), bf16[32,208,128]{2,1,0:T(8,128)(2,1)S(1)}, u32[]{:S(2)}, u32[]{:S(2)}) async-start(bf16[32,208,128]{2,1,0:T(8,128)(2,1)} %pad.12), calls=%async_computation.1 | async-start | bytes 3407872 | tf_op jit(solution)/shard_map/all_to_all | solution.py:173
  55.6 0.9 fusion.59
  56.6 30.9 %all-to-all-done.1 = bf16[32,208,128]{2,1,0:T(8,128)(2,1)S(1)} async-done(((bf16[32,208,128]{2,1,0:T(8,128)(2,1)}), bf16[32,208,128]{2,1,0:T(8,128)(2,1)S(1)}, u32[]{:S(2)}, u32[]{:S(2)}) %all-to-all-start.1) | async-done | bytes 1703968 | tf_op jit(solution)/shard_map/all_to_all | solution.py:173
  88.9 1.1 slice.184
  90.0 1.5 %reshape.481 = bf16[256,2048]{1,0:T(8,128)(2,1)S(1)} reshape(bf16[32,128,128]{2,1,0:T(8,128)(2,1)} %slice.184) | data formatting | bytes 2097152 | tf_op jit(solution)/shard_map/reshape | solution.py:204
  91.5 1.3 select_reduce_fusion.5
  92.8 1.3 copy.59
  94.9 0.9 select_reduce_fusion
  95.9 1.0 fusion.46
  97.6 0.9 fusion.99
  98.5 0.9 convolution_add_fusion
  100.0 0.9 copy.66
  101.8 7.5 %all-to-all-start.2 = ((bf16[32,48,128]{2,1,0:T(8,128)(2,1)}), bf16[32,48,128]{2,1,0:T(8,128)(2,1)S(1)}, u32[]{:S(2)}, u32[]{:S(2)}) async-start(bf16[32,48,128]{2,1,0:T(8,128)(2,1)} %pad_maximum_fusion.2), calls=%async_computation.2 | async-start | bytes 786432 | tf_op jit(solution)/shard_map/all_to_all | solution.py:211
  109.4 1.5 fusion.16
  110.9 1.1 fusion.19
  112.1 1.5 multiply_convert_fusion.2
  113.6 1.0 slice.196
  114.6 0.8 copy.61
  115.4 1.8 %fusion.52 = f32[256,256]{1,0:T(8,128)} fusion(bf16[256,768]{1,0:T(8,128)(2,1)} %multiply_convert_fusion.2), kind=kOutput, calls=%fused_computation.101 | convolution fusion | flops 16777216 | bytes 393216 | tf_op jit(solution)/shard_map/dot_general | solution.py:38
  117.2 2.6 %all-to-all-done.2 = bf16[32,48,128]{2,1,0:T(8,128)(2,1)S(1)} async-done(((bf16[32,48,128]{2,1,0:T(8,128)(2,1)}), bf16[32,48,128]{2,1,0:T(8,128)(2,1)S(1)}, u32[]{:S(2)}, u32[]{:S(2)}) %all-to-all-start.2) | async-done | bytes 393248 | tf_op jit(solution)/shard_map/all_to_all | solution.py:211
  121.2 1.1 convolution_multiply_fusion.1
  122.3 1.1 convolution_multiply_fusion
  125.0 20.4 %all-gather.1 = f32[16,2,256]{2,1,0:T(2,128)S(1)} all-gather(f32[1,2,256]{2,1,0:T(2,128)S(1)} %maximum_bitcast_fusion), channel_id=2, replica_groups=mesh['ctx'=32,'tp'=16] {'tp'}, dimensions={0}, use_global_device_ids=true | all-gather | bytes 34816 | tf_op jit(solution)/shard_map/all_gather | solution.py:256
  145.5 0.9 fusion.45
  146.4 0.9 multiply_convert_fusion.5
  (196 shorter events, 28.8 us)
Async XLA Ops:
  0.6 29.7 %copy-start.1 = (bf16[256,512]{1,0:T(8,128)(2,1)S(1)}, bf16[256,512]{1,0:T(8,128)(2,1)}, u32[]{:S(2)}) copy-start(bf16[256,512]{1,0:T(8,128)(2,1)} %param.17) | copy-start | bytes 786436
  2.1 23.5 %all-to-all-start = ((bf16[16,16,512]{2,1,0:T(8,128)(2,1)}), bf16[16,16,512]{2,1,0:T(8,128)(2,1)S(1)}, u32[]{:S(2)}, u32[]{:S(2)}) async-start(bf16[16,16,512]{2,1,0:T(8,128)(2,1)} %stack.8), calls=%async_computation | async-start | bytes 524288 | tf_op jit(solution)/shard_map/all_to_all | solution.py:110
  14.6 10.1 %copy-start.32 = (s32[8]{0:T(128)}, s32[8]{0:T(128)S(1)}, u32[]{:S(2)}) copy-start(s32[8]{0:T(128)S(1)} %get-tuple-element.16) | copy-start | bytes 100
  15.6 9.2 %copy-start.36 = (pred[8,32]{1,0:T(8,128)(4,1)}, pred[8,32]{1,0:T(8,128)(4,1)S(1)}, u32[]{:S(2)}) copy-start(pred[8,32]{1,0:T(8,128)(4,1)S(1)} %iota_compare_fusion.14) | copy-start | bytes 772
  15.6 9.1 %copy-start.37 = (pred[8,8]{1,0:T(8,128)(4,1)}, pred[8,8]{1,0:T(8,128)(4,1)S(1)}, u32[]{:S(2)}) copy-start(pred[8,8]{1,0:T(8,128)(4,1)S(1)} %iota_compare_fusion.13) | copy-start | bytes 196
  19.4 7.0 %copy-start.22 = (f32[8,256]{1,0:T(8,128)}, f32[8,256]{1,0:T(8,128)S(1)}, u32[]{:S(2)}) copy-start(f32[8,256]{1,0:T(8,128)S(1)} %get-tuple-element.54) | copy-start | bytes 24580
  26.4 4.0 %collective-permute-start = (bf16[3,768]{1,0:T(4,128)(2,1)S(1)}, bf16[3,768]{1,0:T(4,128)(2,1)S(1)}, u32[]{:S(2)}, u32[]{:S(2)}) collective-permute-start(bf16[3,768]{1,0:T(4,128)(2,1)S(1)} %fusion.90), channel_id=1, source_target_pairs={{0,16},{16,32},{32,48},{48,64},{64,80},{80,96},{96,112},{112,128},... | collective-permute-start | bytes 13832 | tf_op jit(solution)/shard_map/ppermute | solution.py:119
  35.7 11.8 %copy-start.13 = (pred[8,32,8]{2,1,0:T(8,128)(4,1)S(1)}, pred[8,32,8]{2,1,0:T(8,128)(4,1)}, u32[]{:S(2)}) copy-start(pred[8,32,8]{2,1,0:T(8,128)(4,1)} %broadcast_and_fusion) | copy-start | bytes 6148
  35.7 12.5 %copy-start.44 = (s32[64]{0:T(128)S(1)}, s32[64]{0:T(128)}, u32[]{:S(2)}) copy-start(s32[64]{0:T(128)} %param.33) | copy-start | bytes 772
  35.8 13.4 %copy-start.48 = (f32[8,256]{1,0:T(8,128)S(1)}, f32[8,256]{1,0:T(8,128)}, u32[]{:S(2)}) copy-start(f32[8,256]{1,0:T(8,128)} %param.24) | copy-start | bytes 24580
  35.8 17.6 %copy-start = (bf16[256,512]{1,0:T(8,128)(2,1)S(1)}, bf16[256,512]{1,0:T(8,128)(2,1)}, u32[]{:S(2)}) copy-start(bf16[256,512]{1,0:T(8,128)(2,1)} %param.21) | copy-start | bytes 786436
  35.8 51.7 %all-to-all-start.1 = ((bf16[32,208,128]{2,1,0:T(8,128)(2,1)}), bf16[32,208,128]{2,1,0:T(8,128)(2,1)S(1)}, u32[]{:S(2)}, u32[]{:S(2)}) async-start(bf16[32,208,128]{2,1,0:T(8,128)(2,1)} %pad.12), calls=%async_computation.1 | async-start | bytes 3407872 | tf_op jit(solution)/shard_map/all_to_all | solution.py:173
  47.5 8.1 %copy-start.3 = (bf16[256,768]{1,0:T(8,128)(2,1)S(1)}, bf16[256,768]{1,0:T(8,128)(2,1)}, u32[]{:S(2)}) copy-start(bf16[256,768]{1,0:T(8,128)(2,1)} %copy-done.2) | copy-start | bytes 1179652
  98.5 10.8 %copy-start.19 = (f32[768]{0:T(1024)S(1)}, f32[768]{0:T(1024)}, u32[]{:S(2)}) copy-start(f32[768]{0:T(1024)} %copy-done.18) | copy-start | bytes 9220
  98.5 10.8 %copy-start.25 = (s32[256]{0:T(256)S(1)}, s32[256]{0:T(256)}, u32[]{:S(2)}) copy-start(s32[256]{0:T(256)} %copy-done.24) | copy-start | bytes 3076
  99.5 11.4 %copy-start.4 = (bf16[255,768]{1,0:T(8,128)(2,1)S(1)}, bf16[255,768]{1,0:T(8,128)(2,1)}, u32[]{:S(2)}) copy-start(bf16[255,768]{1,0:T(8,128)(2,1)} %fusion.42) | copy-start | bytes 1175044
  99.5 11.4 %copy-start.17 = (f32[768]{0:T(1024)S(1)}, f32[768]{0:T(1024)}, u32[]{:S(2)}) copy-start(f32[768]{0:T(1024)} %copy-done.16) | copy-start | bytes 9220
  101.0 11.0 %copy-start.27 = (f32[768]{0:T(1024)S(1)}, f32[768]{0:T(1024)}, u32[]{:S(2)}) copy-start(f32[768]{0:T(1024)} %copy-done.26) | copy-start | bytes 9220
  101.7 10.3 %copy-start.29 = (f32[768]{0:T(1024)S(1)}, f32[768]{0:T(1024)}, u32[]{:S(2)}) copy-start(f32[768]{0:T(1024)} %copy-done.28) | copy-start | bytes 9220
  101.7 10.3 %copy-start.40 = (s32[6]{0:T(128)S(1)}, s32[6]{0:T(128)}, u32[]{:S(2)}) copy-start(s32[6]{0:T(128)} %get-tuple-element.55) | copy-start | bytes 76
  101.7 10.3 %copy-start.41 = (s32[6]{0:T(128)S(1)}, s32[6]{0:T(128)}, u32[]{:S(2)}) copy-start(s32[6]{0:T(128)} %get-tuple-element.56) | copy-start | bytes 76
  101.7 10.3 %copy-start.45 = (s32[256]{0:T(256)S(1)}, s32[256]{0:T(256)}, u32[]{:S(2)}) copy-start(s32[256]{0:T(256)} %get-tuple-element.43) | copy-start | bytes 3076
  101.7 10.3 %copy-start.46 = (pred[256]{0:T(512)(128)(4,1)S(1)}, pred[256]{0:T(512)(128)(4,1)}, u32[]{:S(2)}) copy-start(pred[256]{0:T(512)(128)(4,1)} %get-tuple-element.37) | copy-start | bytes 772
  101.8 10.3 %copy-start.47 = (pred[256]{0:T(512)(128)(4,1)S(1)}, pred[256]{0:T(512)(128)(4,1)}, u32[]{:S(2)}) copy-start(pred[256]{0:T(512)(128)(4,1)} %get-tuple-element.38) | copy-start | bytes 772
  101.8 18.1 %all-to-all-start.2 = ((bf16[32,48,128]{2,1,0:T(8,128)(2,1)}), bf16[32,48,128]{2,1,0:T(8,128)(2,1)S(1)}, u32[]{:S(2)}, u32[]{:S(2)}) async-start(bf16[32,48,128]{2,1,0:T(8,128)(2,1)} %pad_maximum_fusion.2), calls=%async_computation.2 | async-start | bytes 786432 | tf_op jit(solution)/shard_map/all_to_all | solution.py:211
  113.5 6.6 %copy-start.10 = (f32[256,256]{1,0:T(8,128)S(1)}, f32[256,256]{1,0:T(8,128)}, u32[]{:S(2)}) copy-start(f32[256,256]{1,0:T(8,128)} %fusion.59) | copy-start | bytes 786436
  113.5 6.6 %copy-start.14 = (pred[256,256]{1,0:T(8,128)(4,1)S(1)}, pred[256,256]{1,0:T(8,128)(4,1)}, u32[]{:S(2)}) copy-start(pred[256,256]{1,0:T(8,128)(4,1)} %iota_compare_fusion.5) | copy-start | bytes 196612
  113.5 6.6 %copy-start.23 = (f32[8,256]{1,0:T(8,128)S(1)}, f32[8,256]{1,0:T(8,128)}, u32[]{:S(2)}) copy-start(f32[8,256]{1,0:T(8,128)} %copy-done.22) | copy-start | bytes 24580
  113.5 6.6 %copy-start.33 = (f32[8,256]{1,0:T(8,128)S(1)}, f32[8,256]{1,0:T(8,128)}, u32[]{:S(2)}) copy-start(f32[8,256]{1,0:T(8,128)} %get-tuple-element.31) | copy-start | bytes 24580
  113.5 6.6 %copy-start.49 = (f32[8]{0:T(128)S(1)}, f32[8]{0:T(128)}, u32[]{:S(2)}) copy-start(f32[8]{0:T(128)} %param.28) | copy-start | bytes 100
  124.2 21.2 %copy-start.31 = (f32[512]{0:T(512)S(1)}, f32[512]{0:T(512)}, u32[]{:S(2)}) copy-start(f32[512]{0:T(512)} %param.29) | copy-start | bytes 6148
  124.3 21.2 %copy-start.39 = (pred[256]{0:T(512)(128)(4,1)S(1)}, pred[256]{0:T(512)(128)(4,1)}, u32[]{:S(2)}) copy-start(pred[256]{0:T(512)(128)(4,1)} %copy-done.38) | copy-start | bytes 772
  (23 other events, 57.4 us)
